TPU v7x, 256 devices: a whole 4x4x8 slice. The times are simulated.
256 devices in a mesh: group: 16 (over y_lo, z), fsdp: 16 (over x, y_hi, core).
Axes of the slice: x: 4, y: 4 (y_hi: 2, y_lo: 2; y = y_hi * 2 + y_lo), z: 8, core: 2. Of those that a mesh axis runs over, the one named last changes fastest.
Arguments:
- activations: bfloat16 [65536, 2560], P(('group', 'fsdp')), may hold values from -24 to 24
- cotangent: bfloat16 [65536, 2560], P(('group', 'fsdp')), may hold values from -6 to 6
- token_ids: int32 [65536], P(('group', 'fsdp')), may hold values from -100 to 31999, as said below
- step_count: int32 [1], replicated, may hold values from 0 to 7
- master: float32 [16, 2560, 2560], P('group', 'fsdp'), may hold values from -0.12 to 0.12
- first_moment: bfloat16 [16, 2560, 2560], P('group', 'fsdp'), may hold values from -150 to 150
- second_moment: bfloat16 [16, 2560, 2560], P('group', 'fsdp'), may hold values from 200 to 3200
Outputs:
- output: bfloat16 [65536, 2560], P(('group', 'fsdp'))
- act_grad: bfloat16 [65536, 2560], P(('group', 'fsdp'))
- new_master: float32 [16, 2560, 2560], P('group', 'fsdp')
- new_first: bfloat16 [16, 2560, 2560], P('group', 'fsdp')
- new_second: bfloat16 [16, 2560, 2560], P('group', 'fsdp')
Inputs may be any that keep to these rules, and one draw needn't show every extreme that they name: `token_ids`: token ids of a vocabulary of 32000, or -100 for tokens outside the loss; some token of every draw is -100 and some is 31999.
All inputs are finite; a program needn't handle non-finite values.
Results may differ from a plain program's by a relative error of at most 0.014.
Values may be sent and summed in bfloat16 or wider, within the bound.
No kernel may reach another device: no remote copies, remote signals or barrier semaphores. Data moves between devices by JAX's collectives and lax.ppermute only.
A program may use at most 128 MiB of HBM per device.

v0:
```python
from functools import partial

import jax
import jax.numpy as jnp
from jax import lax
from jax.sharding import PartitionSpec as P

beta_one = 0.9
beta_two = 0.95
learn_rate = 0.002
decay_rate = 0.1
epsilon = 1e-05


def for_sending(shard):

    def short(part):
        return part.astype(jnp.bfloat16) if part.dtype == jnp.float32 else part

    return jax.tree.map(short, shard)


def partner(value, axis, distance):
    mask = 2**distance
    pairs = [(source, source ^ mask) for source in range(lax.axis_size(axis))]
    return lax.ppermute(value, axis, pairs)


def adam_delta(master_rows, first_rows, second_rows, gradient, step_count):
    steps_done = (step_count[0] + 1).astype(jnp.float32)
    first_new = beta_one * first_rows.astype(jnp.float32) + (1.0 - beta_one) * gradient
    second_new = beta_two * second_rows.astype(jnp.float32) + (1.0 - beta_two) * gradient * gradient
    first_hat = first_new / (1.0 - jnp.power(jnp.float32(beta_one), steps_done))
    second_hat = second_new / (1.0 - jnp.power(jnp.float32(beta_two), steps_done))
    delta = learn_rate * (first_hat / (jnp.sqrt(second_hat) + epsilon) + decay_rate * master_rows)
    return (delta, first_new.astype(jnp.bfloat16), second_new.astype(jnp.bfloat16))


def partner_stepped(values, bit_index):
    return jax.tree.map(
        lambda part, own: part.astype(own.dtype),
        partner(for_sending(values), "group", bit_index),
        values,
    )


def shards(activations, cotangent, token_ids, step_count, master, first_moment, second_moment):
    live_grad = jnp.where((token_ids >= 0)[:, None], cotangent, jnp.zeros((), cotangent.dtype))
    local_master = master[0]
    levels = lax.axis_size("group").bit_length() - 1
    bit_index = step_count[0] % levels
    weights = lax.all_gather(local_master.astype(jnp.bfloat16), "fsdp", axis=0, tiled=True)
    output = jnp.dot(activations, weights, preferred_element_type=jnp.float32).astype(jnp.bfloat16)
    act_grad = lax.dot_general(
        live_grad, weights, (((1,), (1,)), ((), ())), preferred_element_type=jnp.float32
    )
    output, act_grad = (output, act_grad.astype(jnp.bfloat16))
    gradient = lax.psum_scatter(
        lax.dot_general(
            activations, live_grad, (((0,), (0,)), ((), ())), preferred_element_type=jnp.float32
        ).astype(jnp.bfloat16),
        "fsdp",
        scatter_dimension=0,
        tiled=True,
    ).astype(jnp.float32)
    delta, first_out, second_out = adam_delta(
        local_master, first_moment[0], second_moment[0], gradient, step_count
    )
    stepped = local_master - delta
    branches = [partial(partner_stepped, bit_index=level) for level in range(levels)]
    stepped_other = lax.switch(bit_index, branches, stepped)
    averaged = 0.5 * (stepped + stepped_other)
    return (output, act_grad, averaged[None], first_out[None], second_out[None])


def solution(mesh):
    return jax.shard_map(
        shards,
        mesh=mesh,
        in_specs=(
            P(("group", "fsdp"), None),
            P(("group", "fsdp"), None),
            P(("group", "fsdp")),
            P(),
            P("group", "fsdp", None),
            P("group", "fsdp", None),
            P("group", "fsdp", None),
        ),
        out_specs=(
            P(("group", "fsdp"), None),
            P(("group", "fsdp"), None),
            P("group", "fsdp", None),
            P("group", "fsdp", None),
            P("group", "fsdp", None),
        ),
        check_vma=False,
    )
```

profile of v0, /device:TPU:1, one launch (start us, length us, event | category | flops | bytes accessed | tf_op | source)
XLA Modules:
  0.0 297.2 jit_solution(3903768618917726166)
XLA Ops:
  7.2 0.0 copy-start
  7.2 0.0 reduce-scatter.4.cloned.1.call-start
  7.2 0.8 broadcast_compare_fusion
  8.0 0.5 copy-done
  8.5 8.2 %fusion = bf16[2560,2560]{0,1:T(8,128)(2,1)} fusion(bf16[256,2560]{1,0:T(8,128)(2,1)S(1)} %copy-done, bf16[256,2560]{1,0:T(8,128)(2,1)} %param.12, pred[256]{0:T(512)(128)(4,1)S(1)} %broadcast_compare_fusion), kind=kOutput, calls=%fused_computation.1 | convolution fusion | flops 3362652160 | bytes 15728896 | tf_op jit(solution)/shard_map/dot_general | solution.py:59
  16.7 17.7 %copy.24 = bf16[2560,2560]{1,0:T(8,128)(2,1)} copy(bf16[2560,2560]{0,1:T(8,128)(2,1)} %fusion) | data formatting | bytes 26214400
  34.4 0.0 copy-start.1
  34.4 0.0 reduce-scatter.4.cloned.1.call-update
  34.4 0.0 all-gather.2.cloned.1.call-start
  34.5 1.4 copy-done.1
  35.8 1.0 bitcast_convert_fusion
  36.8 0.0 all-gather.2.cloned.1.call-update
  37.6 132.4 %reduce-scatter.4.cloned.1.call-done = bf16[160,2560]{1,0:T(8,128)(2,1)} async-done(((bf16[2560,2560]{1,0:T(8,128)(2,1)}), bf16[160,2560]{1,0:T(8,128)(2,1)}) %reduce-scatter.4.cloned.1.call-update) | async-done | bytes 819216 | tf_op jit(solution)/shard_map/reduce_scatter | solution.py:58
  170.0 4.8 %fusion.7 = (bf16[1,160,2560]{2,1,0:T(8,128)(2,1)}, f32[160,2560]{1,0:T(8,128)S(1)}, bf16[1,160,2560]{2,1,0:T(8,128)(2,1)}) fusion(bf16[160,2560]{1,0:T(8,128)(2,1)} %reduce-scatter.4.cloned.1.call-done, bf16[1,160,2560]{2,1,0:T(8,128)(2,1)} %param.17, f32[]{:T(128)S(6)} %sub.22, f32[]{:T(128)S(6)} %sub.21, bf16[1,160,2560]{2,1,0:T(8,128)(2,1)} %param.16, ...), kind=kLoop, calls=%fused_computation.17 | loop fusion | flops 8192000 | bytes 7372808 | tf_op jit(solution)/shard_map/broadcast_in_dim | solution.py:73
  174.7 39.1 %conditional.4 = (f32[160,2560]{1,0:T(8,128)}) conditional(s32[]{:T(128)} %clamp.3, f32[160,2560]{1,0:T(8,128)S(1)} %get-tuple-element.26, f32[160,2560]{1,0:T(8,128)S(1)} %get-tuple-element.26, f32[160,2560]{1,0:T(8,128)S(1)} %get-tuple-element.26, f32[160,2560]{1,0:T(8,128)S(1)} %get-tuple-element.26), branch_computations={%region_1.2_spmd, %region_2.3_spmd, %region_3.4_spmd, %region_4.5_... | conditional | flops 819200 | bytes 8192048
  174.7 0.1 convert_element_type.52
  174.8 2.3 collective-permute-start.1
  177.1 35.3 %collective-permute-done.1 = bf16[160,2560]{1,0:T(8,128)(2,1)S(1)} collective-permute-done((bf16[160,2560]{1,0:T(8,128)(2,1)S(1)}, bf16[160,2560]{1,0:T(8,128)(2,1)S(1)}, u32[]{:S(2)}, u32[]{:S(2)}) %collective-permute-start.1) | collective-permute-done | bytes 819232 | tf_op jit(solution)/shard_map/cond/branch_1_fun/ppermute | solution.py:26
  212.5 1.3 convert_element_type.53
  213.8 2.8 multiply_bitcast_fusion
  216.6 54.6 %all-gather.2.cloned.1.call-done = bf16[2560,2560]{1,0:T(8,128)(2,1)} async-done(((bf16[160,2560]{1,0:T(8,128)(2,1)}), bf16[2560,2560]{1,0:T(8,128)(2,1)}) %all-gather.2.cloned.1.call-update) | async-done | bytes 13107216 | tf_op jit(solution)/shard_map/all_gather | solution.py:52
  271.2 9.8 %convolution_convert_fusion.1 = bf16[256,2560]{1,0:T(8,128)(2,1)} fusion(bf16[2560,2560]{1,0:T(8,128)(2,1)} %all-gather.2.cloned.1.call-done, bf16[256,2560]{1,0:T(8,128)(2,1)} %param.12, pred[256]{0:T(512)(128)(4,1)S(1)} %broadcast_compare_fusion), kind=kOutput, calls=%fused_computation.2 | convolution fusion | flops 3356753920 | bytes 15728896 | tf_op jit(solution)/shard_map/dot_general | solution.py:54
  281.0 9.3 %convolution_convert_fusion.2 = bf16[256,2560]{1,0:T(8,128)(2,1)} fusion(bf16[256,2560]{1,0:T(8,128)(2,1)S(1)} %copy-done, bf16[2560,2560]{1,0:T(8,128)(2,1)} %all-gather.2.cloned.1.call-done), kind=kOutput, calls=%fused_computation.3 | convolution fusion | flops 3356098560 | bytes 15728640 | tf_op jit(solution)/shard_map/dot_general | solution.py:53
Async XLA Ops:
  7.2 1.3 copy-start
  7.2 162.8 %reduce-scatter.4.cloned.1.call-start = ((), (), s32[]{:S(2)}) async-start(), calls=%async_computation.2 | async-start | bytes 13926400 | tf_op jit(solution)/shard_map/reduce_scatter | solution.py:58
  34.4 1.4 copy-start.1
  34.4 236.8 %all-gather.2.cloned.1.call-start = ((), (), s32[]{:S(2)}) async-start(), calls=%async_computation.1 | async-start | bytes 13926400 | tf_op jit(solution)/shard_map/all_gather | solution.py:52
  174.8 37.7 %collective-permute-start.1 = (bf16[160,2560]{1,0:T(8,128)(2,1)S(1)}, bf16[160,2560]{1,0:T(8,128)(2,1)S(1)}, u32[]{:S(2)}, u32[]{:S(2)}) collective-permute-start(bf16[160,2560]{1,0:T(8,128)(2,1)S(1)} %convert_element_type.52), channel_id=1, source_target_pairs={{0,32},{16,48},{32,0},{48,16},{64,96},{80,112},{96,64},{112,80},{1... | collective-permute-start | bytes 2457608 | tf_op jit(solution)/shard_map/cond/branch_1_fun/ppermute | solution.py:26
Sparse Core Ops, SparseCore 0:
  34.5 135.4 reduce-scatter.3
  173.3 97.9 all-gather.1
where the time goes:
time: 298 us; the launch traced here: 297 us
  waiting for transfers between devices  222 us (74%)
  matrix products  27.4 us (9%)
  local copies, waits for them, and re-layouts  19.5 us (7%)
  between operations  14.8 us (5%)
  other arithmetic  10.7 us (4%)
    reduce_scatter x1, waiting for transfers between devices, shards(): lax.psum_scatter(lax.dot_general(activations, live_grad, (((0,), (0,)), (...  132 us
    all_gather x1, waiting for transfers between devices, shards(): lax.all_gather(local_master.astype(jnp.bfloat16), 'fsdp', axis=0, tiled=T...  54.6 us
    ppermute x1, waiting for transfers between devices, partner(): return lax.ppermute(value, axis, pairs)  35.3 us
    unnamed x5, local copies, waits for them, and re-layouts  19.5 us
    dot_general x1, matrix products, shards(): lax.dot_general(live_grad, weights, (((1,), (1,)), ((), ())), preferred_e...  9.84 us
    dot_general x1, matrix products, shards(): jnp.dot(activations, weights, preferred_element_type=jnp.float32)  9.32 us
    dot_general x1, matrix products, shards(): lax.dot_general(activations, live_grad, (((0,), (0,)), ((), ())), preferr...  8.2 us
    broadcast_in_dim x2, other arithmetic, shards(): return (output, act_grad, averaged[None], first_out[None], second_out[None])  7.53 us
  transfers between devices with their start and end apart: 3, of which 3 were waited for; matrix products, arithmetic and copies ran while one was open for 3% of the time, Pallas kernels for 0%

commit v1 on v0

v1 whole, which is shorter than its diff:
```python
from functools import partial

import jax
import jax.numpy as jnp
from jax import lax
from jax.experimental import pallas as pl
from jax.experimental.pallas import tpu as pltpu
from jax.sharding import PartitionSpec as P

beta_one = 0.9
beta_two = 0.95
learn_rate = 0.002
decay_rate = 0.1
epsilon = 1e-05

NX = 4
PIECE = 160
HALF = NX * PIECE

bf16 = jnp.bfloat16
f32 = jnp.float32
SMEM = pl.BlockSpec(memory_space=pltpu.SMEM)
VMEM = pl.BlockSpec(memory_space=pltpu.VMEM)
ANY = pl.BlockSpec(memory_space=pl.ANY)
LIMIT = pltpu.CompilerParams(vmem_limit_bytes=48 * 1024 * 1024)


def along(move):
    pairs = []
    for f in range(16):
        x, h, c = move(f // 4, (f // 2) % 2, f % 2)
        pairs.append((f, (x % 4) * 4 + h * 2 + c))
    return pairs


NEXT = along(lambda x, h, c: (x + 1, h, c))
PREV = along(lambda x, h, c: (x - 1, h, c))
OPPOSITE = along(lambda x, h, c: (x + 2, h, c))
ACROSS = along(lambda x, h, c: (x, 1 - h, c))
DIAGONAL = along(lambda x, h, c: (x, 1 - h, 1 - c))
SIBLING = along(lambda x, h, c: (x, h, 1 - c))


def send(value, pairs):
    return lax.ppermute(value, "fsdp", pairs)


def cost(flops, moved):
    return pl.CostEstimate(flops=1, bytes_accessed=1, transcendentals=0)


def held_until(value, after):
    return pl.pallas_call(
        lambda *refs: None,
        out_shape=jax.ShapeDtypeStruct(value.shape, value.dtype),
        in_specs=[ANY] * (1 + len(after)),
        out_specs=ANY,
        input_output_aliases={0: 0},
        cost_estimate=cost(0, 0),
    )(value, *after)


def row_of(place, h, slot, j):
    x, c = place[0], place[2]
    core = c if slot == 0 else 1 - c
    return pl.multiple_of(lax.rem(x + j, NX) * (4 * PIECE) + h * (2 * PIECE) + core * PIECE, 32)


def prepare_kernel(place, act, cot, live, master, bias, masked, own, sib, other, shard, flipped, ordered):
    h = place[1]
    flipped[...] = act[...].T
    for slot in range(2):
        for j in range(NX):
            start = slot * HALF + j * PIECE
            ordered[pl.ds(start, PIECE), :] = flipped[pl.ds(row_of(place, 1 - h, slot, j), PIECE), :]
            start += 2 * HALF
            ordered[pl.ds(start, PIECE), :] = flipped[pl.ds(row_of(place, h, slot, j), PIECE), :]
    other[...] = ordered[: 2 * HALF, :].T
    own[...] = ordered[2 * HALF : 3 * HALF, :].T
    sib[...] = ordered[3 * HALF :, :].T
    masked[...] = jnp.where(live[...] >= 0, cot[...], jnp.zeros((), bf16))
    shard[...] = master[...].astype(bf16)


def prepare(place, activations, cotangent, token_ids, master, bias):
    rows, wide = activations.shape
    shapes = [(rows, wide), (rows, HALF), (rows, HALF), (rows, 2 * HALF), master.shape]
    return pl.pallas_call(
        prepare_kernel,
        out_shape=[jax.ShapeDtypeStruct(shape, bf16) for shape in shapes],
        in_specs=[SMEM, VMEM, VMEM, VMEM, VMEM, SMEM],
        out_specs=[VMEM] * 5,
        scratch_shapes=[pltpu.VMEM((wide, rows), bf16), pltpu.VMEM((wide, rows), bf16)],
        compiler_params=LIMIT,
        cost_estimate=cost(0, 8 * rows * wide),
    )(place, activations, cotangent, token_ids[:, None], master, bias)


OVER_ROWS = (((0,), (0,)), ((), ()))
OVER_COLUMNS = (((1,), (1,)), ((), ()))


def gradient_kernel(*refs):
    acts, grads, outs = refs[0:4], refs[4:8], refs[-NX:]
    wide = grads[0].shape[1]
    width = wide // 2
    for cols in (slice(0, width), slice(width, wide)):
        total = None
        for act, grad in zip(acts, grads):
            term = lax.dot_general(act[...], grad[:, cols], OVER_ROWS, preferred_element_type=f32)
            total = term if total is None else total + term
        for j in range(NX):
            outs[j][:, cols] = total[j * PIECE : (j + 1) * PIECE].astype(outs[j].dtype)


def gradient_blocks(acts, grads, after):
    rows, wide = grads[0].shape
    first = pl.BlockSpec((rows, HALF), lambda i: (0, 0))
    last = pl.BlockSpec((rows, HALF), lambda i: (0, 1))
    whole = pl.BlockSpec((rows, wide), lambda i: (0, 0))
    out = pl.BlockSpec((PIECE, wide), lambda i: (0, 0))
    return pl.pallas_call(
        gradient_kernel,
        grid=(1,),
        out_shape=[jax.ShapeDtypeStruct((PIECE, wide), f32)]
        + [jax.ShapeDtypeStruct((PIECE, wide), bf16)] * (NX - 1),
        in_specs=[first, first, first, last] + [whole] * 4 + [ANY] * len(after),
        out_specs=[out] * NX,
        compiler_params=LIMIT,
        cost_estimate=cost(8 * HALF * rows * wide, 10_000_000),
    )(*acts, *grads, *after)


def fetch(shards, gathered, sems):
    copies = []
    start = 0
    for i, shard in enumerate(shards):
        to = gathered.at[pl.ds(start, shard.shape[0]), :]
        copies.append(pltpu.make_async_copy(shard, to, sems.at[i]))
        start += shard.shape[0]
    for copy in copies:
        copy.start()
    for copy in copies:
        copy.wait()


def times_weights(flipped, gathered):
    return lax.dot_general(flipped, gathered, (((0,), (0,)), ((), ())), preferred_element_type=f32)


def output_kernel(count, own, sib, other, *refs):
    shards = refs[:count]
    theirs, ours, gathered, sems = refs[-4:]
    fetch(shards, gathered, sems)
    theirs[...] = jnp.dot(other[...], gathered[...], preferred_element_type=f32).astype(bf16)
    total = jnp.dot(own[...], gathered[:HALF, :], preferred_element_type=f32)
    ours[...] = total + jnp.dot(sib[...], gathered[HALF:, :], preferred_element_type=f32)


def output_parts(own, sib, other, weights):
    rows, depth = other.shape
    wide = weights[0].shape[1]
    return pl.pallas_call(
        partial(output_kernel, len(weights)),
        out_shape=[jax.ShapeDtypeStruct((rows, wide), bf16), jax.ShapeDtypeStruct((rows, wide), f32)],
        in_specs=[VMEM] * 3 + [ANY] * len(weights),
        out_specs=[VMEM] * 2,
        scratch_shapes=[pltpu.VMEM((depth, wide), bf16), pltpu.SemaphoreType.DMA((len(weights),))],
        compiler_params=LIMIT,
        cost_estimate=cost(4 * depth * rows * wide, 2 * depth * wide + 8 * rows * wide),
    )(own, sib, other, *weights)


def act_grad_kernel(count, masked, across, *refs):
    shards = refs[:count]
    theirs, ours, gathered, sems = refs[-4:]
    fetch(shards, gathered, sems)
    for out, grad in ((theirs, across), (ours, masked)):
        back = lax.dot_general(gathered[...], grad[...], OVER_COLUMNS, preferred_element_type=f32)
        out[...] = back.astype(bf16)


def act_grad_parts(masked, across, weights, after):
    rows, wide = masked.shape
    depth = 2 * HALF
    return pl.pallas_call(
        partial(act_grad_kernel, len(weights)),
        out_shape=[jax.ShapeDtypeStruct((depth, rows), bf16)] * 2,
        in_specs=[VMEM] * 2 + [ANY] * (len(weights) + len(after)),
        out_specs=[VMEM] * 2,
        scratch_shapes=[pltpu.VMEM((depth, wide), bf16), pltpu.SemaphoreType.DMA((len(weights),))],
        compiler_params=LIMIT,
        cost_estimate=cost(4 * depth * rows * wide, 2 * depth * wide + 6 * rows * wide),
    )(masked, across, *weights, *after)


def assemble_kernel(place, ours, theirs, *refs):
    out, flipped = refs[-2:]
    h = place[1]
    for slot in range(2):
        for j in range(NX):
            start = slot * HALF + j * PIECE
            flipped[pl.ds(row_of(place, h, slot, j), PIECE), :] = ours[start : start + PIECE, :]
            flipped[pl.ds(row_of(place, 1 - h, slot, j), PIECE), :] = theirs[start : start + PIECE, :]
    out[...] = flipped[...].T


def assemble(place, ours, theirs, after):
    depth, rows = ours.shape
    return pl.pallas_call(
        assemble_kernel,
        out_shape=jax.ShapeDtypeStruct((rows, 2 * depth), bf16),
        in_specs=[SMEM, VMEM, VMEM] + [ANY] * len(after),
        out_specs=VMEM,
        scratch_shapes=[pltpu.VMEM((2 * depth, rows), bf16)],
        compiler_params=LIMIT,
        cost_estimate=cost(0, 8 * rows * depth),
    )(place, ours, theirs, *after)


def adam_kernel(bias, master, first, second, here, *refs):
    arrived = refs[: NX - 1]
    stepped, sent, first_out, second_out = refs[-4:]
    gradient = here[...]
    for part in arrived:
        gradient += part[...].astype(f32)
    rows = master[...]
    first_new = beta_one * first[...].astype(f32) + (1.0 - beta_one) * gradient
    second_new = beta_two * second[...].astype(f32) + (1.0 - beta_two) * gradient * gradient
    first_hat = first_new / bias[0]
    second_hat = second_new / bias[1]
    delta = learn_rate * (first_hat / (jnp.sqrt(second_hat) + epsilon) + decay_rate * rows)
    stepped[...] = rows - delta
    sent[...] = (rows - delta).astype(bf16)
    first_out[...] = first_new.astype(bf16)
    second_out[...] = second_new.astype(bf16)


def adam(bias, master, first, second, parts):
    rows, wide = master.shape
    steps = 5
    part = pl.BlockSpec((rows // steps, wide), lambda i: (i, 0))
    return pl.pallas_call(
        adam_kernel,
        grid=(steps,),
        out_shape=[jax.ShapeDtypeStruct((rows, wide), f32)] + [jax.ShapeDtypeStruct((rows, wide), bf16)] * 3,
        in_specs=[SMEM] + [part] * (3 + len(parts)),
        out_specs=[part] * 4,
        compiler_params=LIMIT,
        cost_estimate=cost(20 * rows * wide, 26 * rows * wide),
    )(bias, master, first, second, *parts)


def finish_kernel(base, arrived, stepped, other, output, averaged):
    output[...] = (base[...] + arrived[...].astype(f32)).astype(bf16)
    averaged[...] = 0.5 * (stepped[...] + other[...].astype(f32))


def finish(base, arrived, stepped, other):
    rows, wide = base.shape
    mine = stepped.shape[0]
    steps = 5
    cols = pl.BlockSpec((rows, wide // steps), lambda i: (0, i))
    part = pl.BlockSpec((mine // steps, wide), lambda i: (i, 0))
    return pl.pallas_call(
        finish_kernel,
        grid=(steps,),
        out_shape=[jax.ShapeDtypeStruct((rows, wide), bf16), jax.ShapeDtypeStruct((mine, wide), f32)],
        in_specs=[cols, cols, part, part],
        out_specs=[cols, part],
        compiler_params=LIMIT,
        cost_estimate=cost(4 * rows * wide, 14 * rows * wide),
    )(base, arrived, stepped, other)


def from_partner(value, bit_index):
    mask = 2**bit_index
    pairs = [(source, source ^ mask) for source in range(lax.axis_size("group"))]
    return lax.ppermute(value, "group", pairs)


def exchange(sent, beside, bit_index):
    levels = lax.axis_size("group").bit_length() - 1

    def branch(level, value, rest):
        return from_partner(value, level), [send(part, pairs) for part, pairs in zip(rest, moves)]

    rest, moves = [part for part, _ in beside], [pairs for _, pairs in beside]
    return lax.switch(bit_index, [partial(branch, level) for level in range(levels)], sent, rest)


def shards(activations, cotangent, token_ids, step_count, master, first_moment, second_moment):
    master, first_old, second_old = master[0], first_moment[0], second_moment[0]
    levels = lax.axis_size("group").bit_length() - 1
    bit_index = step_count[0] % levels
    f = lax.axis_index("fsdp")
    place = jnp.stack([f // 4, (f // 2) % 2, f % 2]).astype(jnp.int32)
    steps_done = (step_count[0] + 1).astype(f32)
    bias = jnp.stack([1.0 - jnp.power(f32(beta_one), steps_done), 1.0 - jnp.power(f32(beta_two), steps_done)])

    masked, own, sib, other, shard = prepare(place, activations, cotangent, token_ids, master, bias)
    across_act, across = send(other, ACROSS), send(masked, ACROSS)
    pieces = [shard, send(shard, PREV), send(shard, OPPOSITE), send(shard, NEXT)]
    weights = pieces + [send(part, SIBLING) for part in pieces]
    output, base = output_parts(own, sib, across_act, weights)
    output = send(output, ACROSS)
    across = held_until(across, [base])
    acts = [own, send(sib, SIBLING), across_act, send(across_act, SIBLING)]
    grads = [masked, send(masked, SIBLING), across, send(across, SIBLING)]

    here, *away = gradient_blocks(acts, grads, [base])
    away = [send(part, pairs) for part, pairs in zip(away, (NEXT, OPPOSITE, PREV))]
    theirs, ours = act_grad_parts(masked, across, weights, [here])
    stepped, sent, first_out, second_out = adam(bias, master, first_old, second_old, [here, *away])
    arrived, (theirs,) = exchange(sent, [(theirs, ACROSS)], bit_index)
    act_grad = assemble(place, ours, theirs, [])
    output, averaged = finish(base, output, stepped, arrived)
    return (output, act_grad, averaged[None], first_out[None], second_out[None])


def solution(mesh):
    rows = P(("group", "fsdp"), None)
    state = P("group", "fsdp", None)
    return jax.shard_map(
        shards,
        mesh=mesh,
        in_specs=(rows, rows, P(("group", "fsdp")), P(), state, state, state),
        out_specs=(rows, rows, state, state, state),
        check_vma=False,
    )
```

time: 298 us -> 169 us (0.57)
  waiting for transfers between devices: 222 us -> 88.8 us
  Pallas kernels: 0 us -> 37.6 us
  matrix products: 27.4 us -> 0 us
  starting transfers between devices: 2.39 us -> 27.2 us
  between operations: 14.8 us -> 1.6 us
  other arithmetic: 10.7 us -> 0.15 us
  local copies, waits for them, and re-layouts: 19.5 us -> 12.4 us
    reduce_scatter x1 -> x0, waiting for transfers between devices: 132 us -> none  [shards(): lax.psum_scatter(lax.dot_general(activations, live_grad, (((0,), (0,)), (...]
    all_gather x1 -> x0, waiting for transfers between devices: 54.6 us -> none  [shards(): lax.all_gather(local_master.astype(jnp.bfloat16), 'fsdp', axis=0, tiled=T...]
    ppermute x1 -> x19, waiting for transfers between devices: 35.3 us -> 88.8 us  [the longest x18 69.9 us: send(): return lax.ppermute(value, 'fsdp', pairs)]
    pallas_call x0 -> x8, Pallas kernels: none -> 37.6 us  [the longest x1 7.61 us: gradient_blocks(): pl.pallas_call(gradient_kernel, grid=(1,), out_shape=[jax.ShapeDtypeStruc...]
    dot_general x3 -> x0, matrix products: 27.4 us -> none  [the longest x1 9.84 us: shards(): lax.dot_general(live_grad, weights, (((1,), (1,)), ((), ())), preferred_e...]
    ppermute x1 -> x19, starting transfers between devices: 2.31 us -> 27.2 us  [the longest x18 24.1 us: send(): return lax.ppermute(value, 'fsdp', pairs)]
    unnamed x5 -> x46, local copies, waits for them, and re-layouts: 19.5 us -> 11.6 us
    broadcast_in_dim x2 -> x0, other arithmetic: 7.53 us -> none  [shards(): return (output, act_grad, averaged[None], first_out[None], second_out[None])]
  transfers between devices with their start and end apart: 3 -> 19, of which waited for: 3 -> 9; matrix products, arithmetic and copies ran while one was open for 3% -> 0% of each run, Pallas kernels for 0% -> 18%
where the time goes in v1:
time: 169 us; the launch traced here: 168 us
  waiting for transfers between devices  88.8 us (53%)
  Pallas kernels  37.6 us (22%)
  starting transfers between devices  27.2 us (16%)
  local copies, waits for them, and re-layouts  12.4 us (7%)
    ppermute x18, waiting for transfers between devices, send(): return lax.ppermute(value, 'fsdp', pairs)  69.9 us
    ppermute x18, starting transfers between devices, send(): return lax.ppermute(value, 'fsdp', pairs)  24.1 us
    ppermute x1, waiting for transfers between devices, from_partner(): return lax.ppermute(value, 'group', pairs)  18.9 us
    unnamed x46, local copies, waits for them, and re-layouts  11.6 us
    pallas_call x1, Pallas kernels, gradient_blocks(): pl.pallas_call(gradient_kernel, grid=(1,), out_shape=[jax.ShapeDtypeStruc...  7.61 us
    pallas_call x1, Pallas kernels, act_grad_parts(): pl.pallas_call(partial(act_grad_kernel, len(weights)), out_shape=[jax.Sha...  7.45 us
    pallas_call x1, Pallas kernels, output_parts(): pl.pallas_call(partial(output_kernel, len(weights)), out_shape=[jax.Shape...  7.43 us
    pallas_call x1, Pallas kernels, adam(): pl.pallas_call(adam_kernel, grid=(steps,), out_shape=[jax.ShapeDtypeStruc...  5.2 us
  transfers between devices with their start and end apart: 19, of which 9 were waited for; matrix products, arithmetic and copies ran while one was open for 0% of the time, Pallas kernels for 18%

profile of v1, /device:TPU:1, one launch (start us, length us, event | category | flops | bytes accessed | tf_op | source)
XLA Modules:
  0.0 167.8 jit_solution(9908176718908128600)
XLA Ops:
  5.0 2.4 %shard_map.110 = (bf16[256,2560]{1,0:T(8,128)(2,1)S(1)}, bf16[256,640]{1,0:T(8,128)(2,1)S(1)}, bf16[256,640]{1,0:T(8,128)(2,1)S(1)}, bf16[256,1280]{1,0:T(8,128)(2,1)S(1)}, bf16[160,2560]{1,0:T(8,128)(2,1)S(1)}) custom-call(s32[3]{0:T(128)S(1)} %pad_add_fusion.place, bf16[256,2560]{1,0:T(8,128)(2,1)S(1)} %copy-done.12, bf16[256,2560]{1,0:T(8,128)(2,1)S(1)} %copy-done.13, ...), custom_call_target="tpu_custom_call" | custom-call | flops 1 | bytes 1 | tf_op jit(solution)/shard_map/pallas_call | solution.py:88
  7.5 2.1 %collective-permute-start.11 = (bf16[160,2560]{1,0:T(8,128)(2,1)S(1)}, bf16[160,2560]{1,0:T(8,128)(2,1)S(1)}, u32[]{:S(2)}, u32[]{:S(2)}) collective-permute-start(bf16[160,2560]{1,0:T(8,128)(2,1)S(1)} %get-tuple-element.53.refs_0_), channel_id=1, source_target_pairs={{0,4},{1,5},{2,6},{3,7},{4,8},{5,9},{6,10},{7,11},{8,12},{9,13},{1... | collective-permute-start | bytes 2457608 | tf_op jit(solution)/shard_map/ppermute | solution.py:45
  9.6 2.5 %collective-permute-start.10 = (bf16[160,2560]{1,0:T(8,128)(2,1)S(1)}, bf16[160,2560]{1,0:T(8,128)(2,1)S(1)}, u32[]{:S(2)}, u32[]{:S(2)}) collective-permute-start(bf16[160,2560]{1,0:T(8,128)(2,1)S(1)} %get-tuple-element.53.refs_0_), channel_id=1, source_target_pairs={{0,8},{1,9},{2,10},{3,11},{4,12},{5,13},{6,14},{7,15},{8,0},{9,1},... | collective-permute-start | bytes 2457608 | tf_op jit(solution)/shard_map/ppermute | solution.py:45
  13.2 2.9 %collective-permute-start.8 = (bf16[256,1280]{1,0:T(8,128)(2,1)S(1)}, bf16[256,1280]{1,0:T(8,128)(2,1)S(1)}, u32[]{:S(2)}, u32[]{:S(2)}) collective-permute-start(bf16[256,1280]{1,0:T(8,128)(2,1)S(1)} %get-tuple-element.52), channel_id=1, source_target_pairs={{0,2},{1,3},{2,0},{3,1},{4,6},{5,7},{6,4},{7,5},{8,10},{9,11},{10,... | collective-permute-start | bytes 1966088 | tf_op jit(solution)/shard_map/ppermute | solution.py:45
  16.2 13.2 %collective-permute-done.8.other.refs_2_ = bf16[256,1280]{1,0:T(8,128)(2,1)S(1)} collective-permute-done((bf16[256,1280]{1,0:T(8,128)(2,1)S(1)}, bf16[256,1280]{1,0:T(8,128)(2,1)S(1)}, u32[]{:S(2)}, u32[]{:S(2)}) %collective-permute-start.8) | collective-permute-done | bytes 655392 | tf_op jit(solution)/shard_map/ppermute | solution.py:45
  29.4 4.5 %collective-permute-start.12 = (bf16[160,2560]{1,0:T(8,128)(2,1)S(1)}, bf16[160,2560]{1,0:T(8,128)(2,1)S(1)}, u32[]{:S(2)}, u32[]{:S(2)}) collective-permute-start(bf16[160,2560]{1,0:T(8,128)(2,1)S(1)} %get-tuple-element.53.refs_0_), channel_id=1, source_target_pairs={{0,1},{1,0},{2,3},{3,2},{4,5},{5,4},{6,7},{7,6},{8,9},{9,8},{10,11... | collective-permute-start | bytes 2457608 | tf_op jit(solution)/shard_map/ppermute | solution.py:45
  34.0 13.3 %collective-permute-done.10.refs_2_ = bf16[160,2560]{1,0:T(8,128)(2,1)S(1)} collective-permute-done((bf16[160,2560]{1,0:T(8,128)(2,1)S(1)}, bf16[160,2560]{1,0:T(8,128)(2,1)S(1)}, u32[]{:S(2)}, u32[]{:S(2)}) %collective-permute-start.10) | collective-permute-done | bytes 819232 | tf_op jit(solution)/shard_map/ppermute | solution.py:45
  47.2 1.5 collective-permute-start.14
  50.8 2.3 %collective-permute-done.13.refs_5_ = bf16[160,2560]{1,0:T(8,128)(2,1)S(1)} collective-permute-done((bf16[160,2560]{1,0:T(8,128)(2,1)S(1)}, bf16[160,2560]{1,0:T(8,128)(2,1)S(1)}, u32[]{:S(2)}, u32[]{:S(2)}) %collective-permute-start.13) | collective-permute-done | bytes 819232 | tf_op jit(solution)/shard_map/ppermute | solution.py:45
  53.1 7.4 %shard_map.111 = (bf16[256,2560]{1,0:T(8,128)(2,1)}, f32[256,2560]{1,0:T(8,128)}) custom-call(bf16[256,640]{1,0:T(8,128)(2,1)S(1)} %get-tuple-element.50.own.refs_0_, bf16[256,640]{1,0:T(8,128)(2,1)S(1)} %get-tuple-element.51.sib, bf16[256,1280]{1,0:T(8,128)(2,1)S(1)} %collective-permute-done.8.other.refs_2_, ...), custom_call_target="tpu_custom_call" | custom-call | flops 1 | bytes 1 | tf_op jit(solution)/shard_map/pallas_call | solution.py:163
  62.2 2.9 %collective-permute-start.16 = (bf16[256,2560]{1,0:T(8,128)(2,1)}, bf16[256,2560]{1,0:T(8,128)(2,1)}, u32[]{:S(2)}, u32[]{:S(2)}) collective-permute-start(bf16[256,2560]{1,0:T(8,128)(2,1)} %get-tuple-element.55), channel_id=1, source_target_pairs={{0,2},{1,3},{2,0},{3,1},{4,6},{5,7},{6,4},{7,5},{8,10},{9,11},{10,... | collective-permute-start | bytes 3932168 | tf_op jit(solution)/shard_map/ppermute | solution.py:45
  65.8 1.5 collective-permute-done.17.refs_1_
  69.5 7.6 %shard_map.113 = (f32[160,2560]{1,0:T(8,128)}, bf16[160,2560]{1,0:T(8,128)(2,1)}, bf16[160,2560]{1,0:T(8,128)(2,1)}, bf16[160,2560]{1,0:T(8,128)(2,1)}) custom-call(bf16[256,640]{1,0:T(8,128)(2,1)S(1)} %get-tuple-element.50.own.refs_0_, bf16[256,640]{1,0:T(8,128)(2,1)S(1)} %collective-permute-done.17.refs_1_, bf16[256,1280]{1,0:T(8,128)(2,1)S(1)} %copy-done.11, ...), custom_call_target="tpu_custom_call" | custom-call | flops 1 | bytes 1 | tf_op jit(solution)/shard_map/pallas_call | solution.py:122
  78.0 1.7 %collective-permute-start.24 = (bf16[160,2560]{1,0:T(8,128)(2,1)}, bf16[160,2560]{1,0:T(8,128)(2,1)}, u32[]{:S(2)}, u32[]{:S(2)}) collective-permute-start(bf16[160,2560]{1,0:T(8,128)(2,1)} %get-tuple-element.60), channel_id=1, source_target_pairs={{0,12},{1,13},{2,14},{3,15},{4,0},{5,1},{6,2},{7,3},{8,4},{9,5},{1... | collective-permute-start | bytes 2457608 | tf_op jit(solution)/shard_map/ppermute | solution.py:45
  84.3 7.5 %shard_map.115 = (bf16[1280,256]{1,0:T(8,128)(2,1)S(1)}, bf16[1280,256]{1,0:T(8,128)(2,1)S(1)}) custom-call(bf16[256,2560]{1,0:T(8,128)(2,1)} %copy-done.1, bf16[256,2560]{1,0:T(8,128)(2,1)} %shard_map.112.refs_6_.across, bf16[160,2560]{1,0:T(8,128)(2,1)S(1)} %get-tuple-element.53.refs_0_, bf16[160,2560]{1,0:T(8,128)(2,1)S(1)} %copy-done.5, ...), custom_call_target="tpu_custom_call" | custom-call | flops 1 | bytes 1 | tf_op jit(solution)/shard_map/pallas_call | solution.py:186
  91.8 23.7 %collective-permute-done.22.refs_0_ = bf16[160,2560]{1,0:T(8,128)(2,1)S(1)} collective-permute-done((bf16[160,2560]{1,0:T(8,128)(2,1)}, bf16[160,2560]{1,0:T(8,128)(2,1)S(1)}, u32[]{:S(2)}, u32[]{:S(2)}) %collective-permute-start.22) | collective-permute-done | bytes 819232 | tf_op jit(solution)/shard_map/ppermute | solution.py:45
  116.0 5.2 %shard_map.114 = (f32[160,2560]{1,0:T(8,128)S(1)}, bf16[160,2560]{1,0:T(8,128)(2,1)S(1)}, bf16[160,2560]{1,0:T(8,128)(2,1)}, bf16[160,2560]{1,0:T(8,128)(2,1)}) custom-call(f32[2]{0:T(128)S(1)} %pad_maximum_fusion.bias, f32[160,2560]{1,0:T(8,128)} %bitcast.20, bf16[160,2560]{1,0:T(8,128)(2,1)S(1)} %bitcast.17, bf16[160,2560]{1,0:T(8,128)(2,1)S(1)} %bitcast.18, ...), custom_call_target="tpu_custom_call" | custom-call | flops 1 | bytes 1 | tf_op jit(solution)/shard_map/pallas_call | solution.py:243
  121.2 38.0 %conditional.1 = (bf16[160,2560]{1,0:T(8,128)(2,1)}, bf16[1280,256]{1,0:T(8,128)(2,1)}) conditional(s32[]{:T(128)} %clamp.3, (bf16[160,2560]{1,0:T(8,128)(2,1)S(1)}, bf16[1280,256]{1,0:T(8,128)(2,1)S(1)}) %tuple.24, (bf16[160,2560]{1,0:T(8,128)(2,1)S(1)}, bf16[1280,256]{1,0:T(8,128)(2,1)S(1)}) %tuple.24, ...), branch_computations={%region_0.1_spmd, %region_1.2_spmd, %region_2.3_spmd, %region_3.4_... | conditional | bytes 5898336 | solution.py:289
  121.2 3.1 %collective-permute-start.2 = (bf16[160,2560]{1,0:T(8,128)(2,1)S(1)}, bf16[160,2560]{1,0:T(8,128)(2,1)}, u32[]{:S(2)}, u32[]{:S(2)}) collective-permute-start(bf16[160,2560]{1,0:T(8,128)(2,1)S(1)} %get-tuple-element.18), channel_id=1, source_target_pairs={{0,32},{16,48},{32,0},{48,16},{64,96},{80,112},{96,64},{112,80},{1... | collective-permute-start | bytes 2457608 | tf_op jit(solution)/shard_map/cond/branch_1_fun/ppermute | solution.py:279
  124.2 2.0 %collective-permute-start.3 = (bf16[1280,256]{1,0:T(8,128)(2,1)S(1)}, bf16[1280,256]{1,0:T(8,128)(2,1)}, u32[]{:S(2)}, u32[]{:S(2)}) collective-permute-start(bf16[1280,256]{1,0:T(8,128)(2,1)S(1)} %get-tuple-element.19), channel_id=1, source_target_pairs={{0,2},{1,3},{2,0},{3,1},{4,6},{5,7},{6,4},{7,5},{8,10},{9,11},{10,... | collective-permute-start | bytes 1966088 | tf_op jit(solution)/shard_map/cond/branch_1_fun/ppermute | solution.py:45
  126.2 14.0 %collective-permute-done.3 = bf16[1280,256]{1,0:T(8,128)(2,1)} collective-permute-done((bf16[1280,256]{1,0:T(8,128)(2,1)S(1)}, bf16[1280,256]{1,0:T(8,128)(2,1)}, u32[]{:S(2)}, u32[]{:S(2)}) %collective-permute-start.3) | collective-permute-done | bytes 655392 | tf_op jit(solution)/shard_map/cond/branch_1_fun/ppermute | solution.py:45
  140.3 18.9 %collective-permute-done.2 = bf16[160,2560]{1,0:T(8,128)(2,1)} collective-permute-done((bf16[160,2560]{1,0:T(8,128)(2,1)S(1)}, bf16[160,2560]{1,0:T(8,128)(2,1)}, u32[]{:S(2)}, u32[]{:S(2)}) %collective-permute-start.2) | collective-permute-done | bytes 819232 | tf_op jit(solution)/shard_map/cond/branch_1_fun/ppermute | solution.py:279
  160.2 2.8 %shard_map.117 = bf16[256,2560]{1,0:T(8,128)(2,1)} custom-call(s32[3]{0:T(128)S(1)} %pad_add_fusion.place, bf16[1280,256]{1,0:T(8,128)(2,1)S(1)} %copy-done.17, bf16[1280,256]{1,0:T(8,128)(2,1)} %get-tuple-element.67.theirs), custom_call_target="tpu_custom_call" | custom-call | flops 1 | bytes 1 | tf_op jit(solution)/shard_map/pallas_call | solution.py:210
  163.0 4.7 %shard_map.116 = (bf16[256,2560]{1,0:T(8,128)(2,1)}, f32[160,2560]{1,0:T(8,128)}) custom-call(f32[256,2560]{1,0:T(8,128)S(1)} %copy-done, bf16[256,2560]{1,0:T(8,128)(2,1)} %collective-permute-done.16.arrived, f32[160,2560]{1,0:T(8,128)S(1)} %get-tuple-element.61.stepped, bf16[160,2560]{1,0:T(8,128)(2,1)} %get-tuple-element.64.other), custom_call_target="tpu_custom_call" | custom-call | flops 1 | bytes 1 | tf_op jit(solution)/shard_map/pallas_call | solution.py:265
  (72 shorter events, 18.4 us)
Async XLA Ops:
  7.5 53.1 %copy-start.18 = (bf16[256,640]{1,0:T(8,128)(2,1)}, bf16[256,640]{1,0:T(8,128)(2,1)S(1)}, u32[]{:S(2)}) copy-start(bf16[256,640]{1,0:T(8,128)(2,1)S(1)} %get-tuple-element.51.sib) | copy-start | bytes 983044
  7.5 59.8 %copy-start.1 = (bf16[256,2560]{1,0:T(8,128)(2,1)}, bf16[256,2560]{1,0:T(8,128)(2,1)S(1)}, u32[]{:S(2)}) copy-start(bf16[256,2560]{1,0:T(8,128)(2,1)S(1)} %get-tuple-element.56.refs_4_.masked) | copy-start | bytes 3932164
  7.5 26.4 %collective-permute-start.11 = (bf16[160,2560]{1,0:T(8,128)(2,1)S(1)}, bf16[160,2560]{1,0:T(8,128)(2,1)S(1)}, u32[]{:S(2)}, u32[]{:S(2)}) collective-permute-start(bf16[160,2560]{1,0:T(8,128)(2,1)S(1)} %get-tuple-element.53.refs_0_), channel_id=1, source_target_pairs={{0,4},{1,5},{2,6},{3,7},{4,8},{5,9},{6,10},{7,11},{8,12},{9,13},{1... | collective-permute-start | bytes 2457608 | tf_op jit(solution)/shard_map/ppermute | solution.py:45
  9.6 37.7 %collective-permute-start.10 = (bf16[160,2560]{1,0:T(8,128)(2,1)S(1)}, bf16[160,2560]{1,0:T(8,128)(2,1)S(1)}, u32[]{:S(2)}, u32[]{:S(2)}) collective-permute-start(bf16[160,2560]{1,0:T(8,128)(2,1)S(1)} %get-tuple-element.53.refs_0_), channel_id=1, source_target_pairs={{0,8},{1,9},{2,10},{3,11},{4,12},{5,13},{6,14},{7,15},{8,0},{9,1},... | collective-permute-start | bytes 2457608 | tf_op jit(solution)/shard_map/ppermute | solution.py:45
  12.0 36.8 %collective-permute-start.9 = (bf16[160,2560]{1,0:T(8,128)(2,1)S(1)}, bf16[160,2560]{1,0:T(8,128)(2,1)S(1)}, u32[]{:S(2)}, u32[]{:S(2)}) collective-permute-start(bf16[160,2560]{1,0:T(8,128)(2,1)S(1)} %get-tuple-element.53.refs_0_), channel_id=1, source_target_pairs={{0,12},{1,13},{2,14},{3,15},{4,0},{5,1},{6,2},{7,3},{8,4},{9,5},{1... | collective-permute-start | bytes 2457608 | tf_op jit(solution)/shard_map/ppermute | solution.py:45
  13.2 16.2 %collective-permute-start.8 = (bf16[256,1280]{1,0:T(8,128)(2,1)S(1)}, bf16[256,1280]{1,0:T(8,128)(2,1)S(1)}, u32[]{:S(2)}, u32[]{:S(2)}) collective-permute-start(bf16[256,1280]{1,0:T(8,128)(2,1)S(1)} %get-tuple-element.52), channel_id=1, source_target_pairs={{0,2},{1,3},{2,0},{3,1},{4,6},{5,7},{6,4},{7,5},{8,10},{9,11},{10,... | collective-permute-start | bytes 1966088 | tf_op jit(solution)/shard_map/ppermute | solution.py:45
  16.1 44.5 %collective-permute-start.20 = (bf16[256,2560]{1,0:T(8,128)(2,1)S(1)}, bf16[256,2560]{1,0:T(8,128)(2,1)S(1)}, u32[]{:S(2)}, u32[]{:S(2)}) collective-permute-start(bf16[256,2560]{1,0:T(8,128)(2,1)S(1)} %get-tuple-element.56.refs_4_.masked), channel_id=1, source_target_pairs={{0,2},{1,3},{2,0},{3,1},{4,6},{5,7},{6,4},{7,5},{8,10},{9,11},{10,... | collective-permute-start | bytes 3932168 | tf_op jit(solution)/shard_map/ppermute | solution.py:45
  29.4 31.1 %copy-start.10 = (bf16[256,1280]{1,0:T(8,128)(2,1)}, bf16[256,1280]{1,0:T(8,128)(2,1)S(1)}, u32[]{:S(2)}) copy-start(bf16[256,1280]{1,0:T(8,128)(2,1)S(1)} %collective-permute-done.8.other.refs_2_) | copy-start | bytes 1966084
  29.4 19.5 %collective-permute-start.12 = (bf16[160,2560]{1,0:T(8,128)(2,1)S(1)}, bf16[160,2560]{1,0:T(8,128)(2,1)S(1)}, u32[]{:S(2)}, u32[]{:S(2)}) collective-permute-start(bf16[160,2560]{1,0:T(8,128)(2,1)S(1)} %get-tuple-element.53.refs_0_), channel_id=1, source_target_pairs={{0,1},{1,0},{2,3},{3,2},{4,5},{5,4},{6,7},{7,6},{8,9},{9,8},{10,11... | collective-permute-start | bytes 2457608 | tf_op jit(solution)/shard_map/ppermute | solution.py:45
  33.9 15.4 %collective-permute-start.15 = (bf16[160,2560]{1,0:T(8,128)(2,1)S(1)}, bf16[160,2560]{1,0:T(8,128)(2,1)S(1)}, u32[]{:S(2)}, u32[]{:S(2)}) collective-permute-start(bf16[160,2560]{1,0:T(8,128)(2,1)S(1)} %collective-permute-done.11.refs_3_), channel_id=1, source_target_pairs={{0,1},{1,0},{2,3},{3,2},{4,5},{5,4},{6,7},{7,6},{8,9},{9,8},{10,11... | collective-permute-start | bytes 2457608 | tf_op jit(solution)/shard_map/ppermute | solution.py:45
  47.2 3.5 %collective-permute-start.14 = (bf16[160,2560]{1,0:T(8,128)(2,1)S(1)}, bf16[160,2560]{1,0:T(8,128)(2,1)S(1)}, u32[]{:S(2)}, u32[]{:S(2)}) collective-permute-start(bf16[160,2560]{1,0:T(8,128)(2,1)S(1)} %collective-permute-done.10.refs_2_), channel_id=1, source_target_pairs={{0,1},{1,0},{2,3},{3,2},{4,5},{5,4},{6,7},{7,6},{8,9},{9,8},{10,11... | collective-permute-start | bytes 2457608 | tf_op jit(solution)/shard_map/ppermute | solution.py:45
  48.8 4.3 %collective-permute-start.13 = (bf16[160,2560]{1,0:T(8,128)(2,1)S(1)}, bf16[160,2560]{1,0:T(8,128)(2,1)S(1)}, u32[]{:S(2)}, u32[]{:S(2)}) collective-permute-start(bf16[160,2560]{1,0:T(8,128)(2,1)S(1)} %collective-permute-done.9.refs_1_), channel_id=1, source_target_pairs={{0,1},{1,0},{2,3},{3,2},{4,5},{5,4},{6,7},{7,6},{8,9},{9,8},{10,11... | collective-permute-start | bytes 2457608 | tf_op jit(solution)/shard_map/ppermute | solution.py:45
  48.9 18.3 %collective-permute-start.19 = (bf16[256,2560]{1,0:T(8,128)(2,1)S(1)}, bf16[256,2560]{1,0:T(8,128)(2,1)}, u32[]{:S(2)}, u32[]{:S(2)}) collective-permute-start(bf16[256,2560]{1,0:T(8,128)(2,1)S(1)} %get-tuple-element.56.refs_4_.masked), channel_id=1, source_target_pairs={{0,1},{1,0},{2,3},{3,2},{4,5},{5,4},{6,7},{7,6},{8,9},{9,8},{10,11... | collective-permute-start | bytes 3932168 | tf_op jit(solution)/shard_map/ppermute | solution.py:45
  61.7 5.6 %collective-permute-start.21 = (bf16[256,2560]{1,0:T(8,128)(2,1)}, bf16[256,2560]{1,0:T(8,128)(2,1)S(1)}, u32[]{:S(2)}, u32[]{:S(2)}) collective-permute-start(bf16[256,2560]{1,0:T(8,128)(2,1)} %shard_map.112.refs_6_.across), channel_id=1, source_target_pairs={{0,1},{1,0},{2,3},{3,2},{4,5},{5,4},{6,7},{7,6},{8,9},{9,8},{10,11... | collective-permute-start | bytes 3932168 | tf_op jit(solution)/shard_map/ppermute | solution.py:45
  62.0 5.2 %collective-permute-start.18 = (bf16[256,1280]{1,0:T(8,128)(2,1)}, bf16[256,1280]{1,0:T(8,128)(2,1)S(1)}, u32[]{:S(2)}, u32[]{:S(2)}) collective-permute-start(bf16[256,1280]{1,0:T(8,128)(2,1)} %copy-done.10), channel_id=1, source_target_pairs={{0,1},{1,0},{2,3},{3,2},{4,5},{5,4},{6,7},{7,6},{8,9},{9,8},{10,11... | collective-permute-start | bytes 1966088 | tf_op jit(solution)/shard_map/ppermute | solution.py:45
  62.2 100.9 %collective-permute-start.16 = (bf16[256,2560]{1,0:T(8,128)(2,1)}, bf16[256,2560]{1,0:T(8,128)(2,1)}, u32[]{:S(2)}, u32[]{:S(2)}) collective-permute-start(bf16[256,2560]{1,0:T(8,128)(2,1)} %get-tuple-element.55), channel_id=1, source_target_pairs={{0,2},{1,3},{2,0},{3,1},{4,6},{5,7},{6,4},{7,5},{8,10},{9,11},{10,... | collective-permute-start | bytes 3932168 | tf_op jit(solution)/shard_map/ppermute | solution.py:45
  65.1 2.1 %collective-permute-start.17 = (bf16[256,640]{1,0:T(8,128)(2,1)}, bf16[256,640]{1,0:T(8,128)(2,1)S(1)}, u32[]{:S(2)}, u32[]{:S(2)}) collective-permute-start(bf16[256,640]{1,0:T(8,128)(2,1)} %copy-done.18), channel_id=1, source_target_pairs={{0,1},{1,0},{2,3},{3,2},{4,5},{5,4},{6,7},{7,6},{8,9},{9,8},{10,11... | collective-permute-start | bytes 983048 | tf_op jit(solution)/shard_map/ppermute | solution.py:45
  77.1 38.4 %collective-permute-start.22 = (bf16[160,2560]{1,0:T(8,128)(2,1)}, bf16[160,2560]{1,0:T(8,128)(2,1)S(1)}, u32[]{:S(2)}, u32[]{:S(2)}) collective-permute-start(bf16[160,2560]{1,0:T(8,128)(2,1)} %get-tuple-element.58), channel_id=1, source_target_pairs={{0,4},{1,5},{2,6},{3,7},{4,8},{5,9},{6,10},{7,11},{8,12},{9,13},{1... | collective-permute-start | bytes 2457608 | tf_op jit(solution)/shard_map/ppermute | solution.py:45
  77.1 38.4 %collective-permute-start.23 = (bf16[160,2560]{1,0:T(8,128)(2,1)}, bf16[160,2560]{1,0:T(8,128)(2,1)S(1)}, u32[]{:S(2)}, u32[]{:S(2)}) collective-permute-start(bf16[160,2560]{1,0:T(8,128)(2,1)} %get-tuple-element.59), channel_id=1, source_target_pairs={{0,8},{1,9},{2,10},{3,11},{4,12},{5,13},{6,14},{7,15},{8,0},{9,1},... | collective-permute-start | bytes 2457608 | tf_op jit(solution)/shard_map/ppermute | solution.py:45
  78.0 37.9 %collective-permute-start.24 = (bf16[160,2560]{1,0:T(8,128)(2,1)}, bf16[160,2560]{1,0:T(8,128)(2,1)}, u32[]{:S(2)}, u32[]{:S(2)}) collective-permute-start(bf16[160,2560]{1,0:T(8,128)(2,1)} %get-tuple-element.60), channel_id=1, source_target_pairs={{0,12},{1,13},{2,14},{3,15},{4,0},{5,1},{6,2},{7,3},{8,4},{9,5},{1... | collective-permute-start | bytes 2457608 | tf_op jit(solution)/shard_map/ppermute | solution.py:45
  84.3 31.6 %copy-start.14 = (bf16[1,160,2560]{2,1,0:T(8,128)(2,1)S(1)}, bf16[1,160,2560]{2,1,0:T(8,128)(2,1)}, u32[]{:S(2)}) copy-start(bf16[1,160,2560]{2,1,0:T(8,128)(2,1)} %param.16) | copy-start | bytes 2457604
  84.3 31.6 %copy-start.15 = (bf16[1,160,2560]{2,1,0:T(8,128)(2,1)S(1)}, bf16[1,160,2560]{2,1,0:T(8,128)(2,1)}, u32[]{:S(2)}) copy-start(bf16[1,160,2560]{2,1,0:T(8,128)(2,1)} %param.17) | copy-start | bytes 2457604
  121.2 38.0 %collective-permute-start.2 = (bf16[160,2560]{1,0:T(8,128)(2,1)S(1)}, bf16[160,2560]{1,0:T(8,128)(2,1)}, u32[]{:S(2)}, u32[]{:S(2)}) collective-permute-start(bf16[160,2560]{1,0:T(8,128)(2,1)S(1)} %get-tuple-element.18), channel_id=1, source_target_pairs={{0,32},{16,48},{32,0},{48,16},{64,96},{80,112},{96,64},{112,80},{1... | collective-permute-start | bytes 2457608 | tf_op jit(solution)/shard_map/cond/branch_1_fun/ppermute | solution.py:279
  124.2 16.1 %collective-permute-start.3 = (bf16[1280,256]{1,0:T(8,128)(2,1)S(1)}, bf16[1280,256]{1,0:T(8,128)(2,1)}, u32[]{:S(2)}, u32[]{:S(2)}) collective-permute-start(bf16[1280,256]{1,0:T(8,128)(2,1)S(1)} %get-tuple-element.19), channel_id=1, source_target_pairs={{0,2},{1,3},{2,0},{3,1},{4,6},{5,7},{6,4},{7,5},{8,10},{9,11},{10,... | collective-permute-start | bytes 1966088 | tf_op jit(solution)/shard_map/cond/branch_1_fun/ppermute | solution.py:45
  (18 other events, 94.1 us)
